TPU v7x, 256 devices: a whole 4x4x8 slice. The times are simulated.
256 devices in a mesh: region: 64 (over x, z, core), ray: 4 (over y).
Axes of the slice: x: 4, y: 4, z: 8, core: 2. Of those that a mesh axis runs over, the one named last changes fastest.
Arguments:
- bricks: bfloat16 [64, 512, 512], P('region', 'ray'), may hold values from -6 to 6
- pair_index: int32 [64, 256, 16], P('region', 'ray'), may hold values from 0 to 511
- interp_weight: bfloat16 [64, 256, 512, 128], P('region', 'ray'), may hold values from 0 to 0.15234375
- step_len: float32 [64, 2, 65536], P('region', None, 'ray'), may hold values from 0.00234375 to 0.09375
- sample_count: int32 [64, 65536], P('region', 'ray'), may hold values from 0 to 2
- w_first: bfloat16 [64, 256], replicated, may hold values from -0.75 to 0.75
- w_second: bfloat16 [256, 256], replicated, may hold values from -0.375 to 0.375
- w_out: bfloat16 [256, 33], replicated, may hold values from -0.375 to 0.375
Outputs:
- color: float32 [32, 65536], P(None, ('ray', 'region'))
- transmittance: float32 [65536], P(('ray', 'region'))
All inputs are finite; a program needn't handle non-finite values.
Results may differ from a plain program's by a relative error of at most 0.0015.
Values may be sent and summed in bfloat16 or wider, within the bound.
A program may use at most 128 MiB of HBM per device.

v0:
```python
import jax
import jax.numpy as jnp
from jax import lax
from jax.sharding import PartitionSpec as P


def swapped(block, axis, distance):
    count = lax.axis_size(axis)
    route = []
    for low in range(count):
        high = low | 1 << distance
        if high != low and high < count:
            route += [(low, high), (high, low)]
    return lax.ppermute(block, axis, route)


def shade(field, steps, counts):
    nfeat = field.shape[0] - 1
    feats = field[:nfeat]
    sigma = jax.nn.softplus(field[nfeat])
    depth = steps.shape[1]
    live = (jnp.arange(depth, dtype=jnp.int32)[None, :] < counts[:, None]).astype(jnp.float32)
    tau = sigma * steps * live
    before = jnp.cumsum(tau, axis=1) - tau
    weights = jnp.exp(-before) * (1.0 - jnp.exp(-tau))
    slab_color = jnp.sum(feats * weights[None, :, :], axis=2)
    slab_trans = jnp.exp(-jnp.sum(tau, axis=1))
    return (slab_color, slab_trans)


def reverse_blocks(values, levels):
    lead = values.shape[:-1]
    block = values.shape[-1] >> levels
    shaped = values.reshape(lead + (2,) * levels + (block,))
    first = len(lead)
    order = (
        tuple(range(first)) + tuple(range(first + levels - 1, first - 1, -1)) + (first + levels,)
    )
    return jnp.transpose(shaped, order).reshape(values.shape)


def shards(bricks, pair_index, interp_weight, step_len, sample_count, w_first, w_second, w_out):
    table = lax.all_gather(bricks[0], "ray", axis=0, tiled=True)
    index = pair_index[0]
    tiles, slots = index.shape
    channels = w_first.shape[0]
    voxels = table.shape[1] // channels
    rows = jnp.take(table, index.reshape(-1), axis=0).reshape(tiles, slots * voxels, channels)
    feats = jnp.einsum("tsk,tkc->cts", interp_weight[0], rows, preferred_element_type=jnp.float32)
    feats = feats.astype(jnp.bfloat16).reshape(channels, -1)
    first = jax.nn.relu(
        jnp.einsum("ch,cs->hs", w_first, feats, preferred_element_type=jnp.float32)
    ).astype(jnp.bfloat16)
    second = jax.nn.relu(
        jnp.einsum("hg,hs->gs", w_second, first, preferred_element_type=jnp.float32)
    ).astype(jnp.bfloat16)
    field = jnp.einsum("hf,hs->fs", w_out, second, preferred_element_type=jnp.float32)
    steps = step_len[0].T
    rays, depth = steps.shape
    field = field.reshape(field.shape[0], rays, depth)
    slab_color, slab_trans = shade(field, steps, sample_count[0])
    groups = lax.axis_size("region")
    levels = groups.bit_length() - 1
    color = reverse_blocks(slab_color, levels)
    trans = reverse_blocks(slab_trans, levels)
    position = lax.axis_index("region")
    for level in range(levels):
        half = color.shape[1] // 2
        front = jnp.bitwise_and(jnp.right_shift(position, level), 1) == 0
        keep_color = jnp.where(front, color[:, :half], color[:, half:])
        send_color = jnp.where(front, color[:, half:], color[:, :half])
        keep_trans = jnp.where(front, trans[:half], trans[half:])
        send_trans = jnp.where(front, trans[half:], trans[:half])
        other_color, other_trans = swapped((send_color, send_trans), "region", level)
        near_color = jnp.where(front, keep_color, other_color)
        near_trans = jnp.where(front, keep_trans, other_trans)
        far_color = jnp.where(front, other_color, keep_color)
        far_trans = jnp.where(front, other_trans, keep_trans)
        color = near_color + near_trans[None, :] * far_color
        trans = near_trans * far_trans
    return (color, trans)


def solution(mesh):
    return jax.shard_map(
        shards,
        mesh=mesh,
        in_specs=(
            P("region", "ray", None),
            P("region", "ray", None),
            P("region", "ray", None, None),
            P("region", None, "ray"),
            P("region", "ray"),
            P(),
            P(),
            P(),
        ),
        out_specs=(P(None, ("ray", "region")), P(("ray", "region"))),
        check_vma=False,
    )
```

profile of v0, /device:TPU:1, one launch (start us, length us, event | category | flops | bytes accessed | tf_op | source)
XLA Modules:
  0.0 282.1 jit_solution(6933370444085144428)
XLA Ops:
  0.6 0.7 compare_and_fusion
  1.4 0.8 copy.34
  2.2 0.1 copy.33
  2.3 0.1 reshape_squeeze.6
  2.4 12.8 %all-gather = bf16[1,512,512]{2,1,0:T(8,128)(2,1)S(1)} all-gather(bf16[1,128,512]{2,1,0:T(8,128)(2,1)} %param.8), channel_id=2, replica_groups=mesh['region'=64,'ray'=4] {'ray'}, dimensions={1}, use_global_device_ids=true | all-gather | bytes 655360 | tf_op jit(solution)/shard_map/all_gather | solution.py:43
  15.2 4.0 %gather_fusion = bf16[1024,512]{1,0:T(8,128)(2,1)S(1)} fusion(bf16[512,512]{1,0:T(8,128)(2,1)S(1)} %bitcast.39, s32[1024]{0:T(1024)S(1)} %broadcast_clamp_fusion), kind=kCustom, calls=%fused_computation | custom fusion | bytes 2101248 | tf_op jit(solution)/shard_map/jit(_take)/gather | solution.py:48
  19.2 1.1 gather.7
  20.3 6.3 %convert_bitcast_fusion = bf16[64,8,8,512]{3,2,1,0:T(8,128)(2,1)S(1)} fusion(bf16[1,64,512,128]{3,2,1,0:T(8,128)(2,1)} %param.10, bf16[64,128,64]{2,1,0:T(8,128)(2,1)S(1)} %gather.7, pred[64,128]{1,0:T(8,128)(4,1)S(1)} %copy.33), kind=kOutput, calls=%fused_computation.14 | convolution fusion | flops 539492352 | bytes 13639680 | tf_op jit(solution)/shard_map/tsk,tkc->cts/dot_general | solution.py:49
  26.6 2.4 copy.46
  28.9 12.5 %fusion = bf16[32768,256]{1,0:T(8,128)(2,1)} fusion(bf16[64,32768]{1,0:T(8,128)(2,1)} %bitcast.42, bf16[64,256]{1,0:T(8,128)(2,1)S(1)} %copy-done.5), kind=kOutput, calls=%fused_computation.3 | convolution fusion | flops 1090519040 | bytes 21004288 | tf_op jit(solution)/shard_map/ch,cs->hs/dot_general | solution.py:52
  41.5 14.2 %convolution_bitcast_fusion = f32[33,32768]{1,0:T(8,128)} fusion(bf16[256,33]{0,1:T(8,128)(2,1)S(1)} %copy-done.6, bf16[32768,256]{1,0:T(8,128)(2,1)} %fusion, bf16[256,256]{1,0:T(8,128)(2,1)S(1)} %copy-done), kind=kOutput, calls=%fused_computation.5 | convolution fusion | flops 4865392640 | bytes 21250560 | tf_op jit(solution)/shard_map/hf,hs->fs/dot_general | solution.py:57
  55.6 1.6 slice_reduce_fusion
  57.2 4.5 %slice.137 = f32[32,32768]{1,0:T(8,128)} slice(f32[33,32768]{1,0:T(8,128)} %convolution_bitcast_fusion), slice={[0:32], [0:32768]} | slice | bytes 8388608 | tf_op jit(solution)/shard_map/slice | solution.py:19
  61.7 4.9 %copy.38 = f32[1,2,16384]{1,2,0:T(8,128)} copy(f32[1,2,16384]{2,1,0:T(2,128)S(1)} %copy-done.3) | data formatting | bytes 262144 | tf_op args[3]
  66.7 9.7 %squeeze.14 = f32[16384,2]{1,0:T(8,128)} reshape(f32[32768]{0:T(1024)S(1)} %slice_reduce_fusion) | data formatting | bytes 262144 | tf_op jit(solution)/shard_map/squeeze | solution.py:20
  76.4 10.5 %fusion.13 = (f32[16384]{0:T(1024)S(1)}, f32[16384,2]{1,0:T(8,128)}) fusion(f32[1,2,16384]{1,2,0:T(8,128)} %copy.38, f32[16384,2]{1,0:T(8,128)} %squeeze.14, s32[16384]{0:T(1024)S(1)} %bitcast.48), kind=kLoop, calls=%fused_computation.63 | loop fusion | flops 311296 | bytes 524288 | tf_op jit(solution)/shard_map/reduce_sum | solution.py:27
  86.9 10.5 %reduce_window_sum.11 = f32[16384,2]{1,0:T(8,128)} reduce-window(f32[16384,2]{1,0:T(8,128)} %get-tuple-element.3, f32[]{:T(128)} %constant.44.clone.1), window={size=1x2 pad=0_0x1_0}, to_apply=%region_0.1 | reduce-window | flops 32768 | bytes 262148 | tf_op jit(solution)/shard_map/jit(cumsum)/reduce_window_sum | solution.py:24
  97.3 9.6 %subtract_multiply_fusion = f32[16384,2]{1,0:T(8,128)} fusion(f32[16384,2]{1,0:T(8,128)} %get-tuple-element.3, f32[16384,2]{1,0:T(8,128)} %reduce_window_sum.11), kind=kLoop, calls=%fused_computation.12 | loop fusion | flops 163840 | bytes 393216 | tf_op jit(solution)/shard_map/mul | solution.py:25
  106.9 10.3 %copy.37 = f32[32,32768]{0,1:T(8,128)} copy(f32[32,32768]{1,0:T(8,128)} %slice.137) | data formatting | bytes 8388608 | tf_op jit(solution)/shard_map/slice | solution.py:19
  117.2 93.2 %multiply_reduce_fusion = f32[32,16384]{0,1:T(8,128)} fusion(f32[32,16384,2]{0,2,1:T(2,128)} %bitcast.40, f32[16384,2]{1,0:T(8,128)} %subtract_multiply_fusion), kind=kLoop, calls=%fused_computation.7 | loop fusion | flops 1572864 | bytes 6422528 | tf_op jit(solution)/shard_map/reduce_sum | solution.py:26
  210.4 8.1 %copy.45 = f32[32,2,2,2,2,2,2,256]{7,1,2,3,4,5,6,0:T(2,128)} copy(f32[32,2,2,2,2,2,2,256]{0,7,6,5,4,3,2,1:T(8,128)} %bitcast.41) | data formatting | bytes 4194304 | tf_op jit(solution)/shard_map/transpose | solution.py:39
  218.5 3.0 %reshape.77 = f32[32,16384]{1,0:T(8,128)S(1)} reshape(f32[32,2,2,2,2,2,2,256]{7,6,5,4,3,2,1,0:T(2,128)} %bitcast.43) | data formatting | bytes 4194304 | tf_op jit(solution)/shard_map/reshape | solution.py:39
  221.5 1.1 slice_select_fusion
  222.6 4.0 %collective-permute-start = (f32[32,8192]{1,0:T(8,128)}, f32[32,8192]{1,0:T(8,128)S(1)}, u32[]{:S(2)}, u32[]{:S(2)}) collective-permute-start(f32[32,8192]{1,0:T(8,128)} %slice_select_fusion), channel_id=1, source_target_pairs={{0,4},{4,0},{8,12},{12,8},{16,20},{20,16},{24,28},{28,24},{32,36},... | collective-permute-start | bytes 3145736 | tf_op jit(solution)/shard_map/ppermute | solution.py:14
  226.8 0.1 collective-permute-start.1
  227.0 2.0 collective-permute-done.1
  229.0 0.1 collective-permute-start.3
  229.1 2.6 collective-permute-done.3
  231.7 1.0 copy-done.2
  232.6 1.4 multiply_add_fusion
  234.0 0.1 slice_select_fusion.1
  234.1 0.3 collective-permute-start.2
  234.4 2.8 collective-permute-start.5
  237.2 7.2 %collective-permute-done.5 = f32[2048]{0:T(1024)S(1)} collective-permute-done((f32[2048]{0:T(1024)S(1)}, f32[2048]{0:T(1024)S(1)}, u32[]{:S(2)}, u32[]{:S(2)}) %collective-permute-start.5) | collective-permute-done | bytes 8224 | tf_op jit(solution)/shard_map/ppermute | solution.py:14
  244.5 5.7 %collective-permute-start.7 = (f32[1024]{0:T(1024)S(1)}, f32[1024]{0:T(1024)S(1)}, u32[]{:S(2)}, u32[]{:S(2)}) collective-permute-start(f32[1024]{0:T(1024)S(1)} %slice_select_fusion.10), channel_id=1, source_target_pairs={{0,32},{32,0},{4,36},{36,4},{8,40},{40,8},{12,44},{44,12},{16,48},... | collective-permute-start | bytes 12296 | tf_op jit(solution)/shard_map/ppermute | solution.py:14
  250.2 0.1 multiply_add_fusion.1
  250.3 2.9 %collective-permute-start.4 = (f32[32,2048]{1,0:T(8,128)S(1)}, f32[32,2048]{1,0:T(8,128)S(1)}, u32[]{:S(2)}, u32[]{:S(2)}) collective-permute-start(f32[32,2048]{1,0:T(8,128)S(1)} %slice_select_fusion.2), channel_id=1, source_target_pairs={{0,16},{16,0},{4,20},{20,4},{8,24},{24,8},{12,28},{28,12},{32,48},... | collective-permute-start | bytes 786440 | tf_op jit(solution)/shard_map/ppermute | solution.py:14
  253.2 1.3 collective-permute-start.9
  254.5 9.5 %collective-permute-done.4 = f32[32,2048]{1,0:T(8,128)S(1)} collective-permute-done((f32[32,2048]{1,0:T(8,128)S(1)}, f32[32,2048]{1,0:T(8,128)S(1)}, u32[]{:S(2)}, u32[]{:S(2)}) %collective-permute-start.4) | collective-permute-done | bytes 262176 | tf_op jit(solution)/shard_map/ppermute | solution.py:14
  264.1 0.1 multiply_add_fusion.2
  264.2 1.6 collective-permute-start.6
  265.8 7.1 %collective-permute-done.6 = f32[32,1024]{1,0:T(8,128)S(1)} collective-permute-done((f32[32,1024]{1,0:T(8,128)S(1)}, f32[32,1024]{1,0:T(8,128)S(1)}, u32[]{:S(2)}, u32[]{:S(2)}) %collective-permute-start.6) | collective-permute-done | bytes 131104 | tf_op jit(solution)/shard_map/ppermute | solution.py:14
  272.9 1.3 collective-permute-start.8
  274.2 2.5 collective-permute-start.11
  276.7 2.3 collective-permute-start.10
  279.0 0.6 select_multiply_fusion.5
  279.6 1.9 collective-permute-done.10
  281.4 0.6 multiply_add_fusion.5
  (45 shorter events, 0.5 us)
Async XLA Ops:
  0.6 40.8 %copy-start = (bf16[256,256]{1,0:T(8,128)(2,1)S(1)}, bf16[256,256]{1,0:T(8,128)(2,1)}, u32[]{:S(2)}) copy-start(bf16[256,256]{1,0:T(8,128)(2,1)} %param.14) | copy-start | bytes 393220
  20.3 8.6 %copy-start.5 = (bf16[64,256]{1,0:T(8,128)(2,1)S(1)}, bf16[64,256]{1,0:T(8,128)(2,1)}, u32[]{:S(2)}) copy-start(bf16[64,256]{1,0:T(8,128)(2,1)} %param.13) | copy-start | bytes 98308
  28.9 12.5 %copy-start.6 = (bf16[256,33]{0,1:T(8,128)(2,1)S(1)}, bf16[256,33]{0,1:T(8,128)(2,1)}, u32[]{:S(2)}) copy-start(bf16[256,33]{0,1:T(8,128)(2,1)} %param.15) | copy-start | bytes 50692
  55.6 6.1 %copy-start.3 = (f32[1,2,16384]{2,1,0:T(2,128)S(1)}, f32[1,2,16384]{2,1,0:T(2,128)}, u32[]{:S(2)}) copy-start(f32[1,2,16384]{2,1,0:T(2,128)} %param.11) | copy-start | bytes 393220
  61.7 14.7 %copy-start.4 = (s32[1,16384]{1,0:T(1,128)S(1)}, s32[1,16384]{1,0:T(1,128)}, u32[]{:S(2)}) copy-start(s32[1,16384]{1,0:T(1,128)} %param.12) | copy-start | bytes 196612
  218.5 63.5 %copy-start.1 = (bf16[256,256]{1,0:T(8,128)(2,1)S(1)}, bf16[256,256]{1,0:T(8,128)(2,1)}, u32[]{:S(2)}) copy-start(bf16[256,256]{1,0:T(8,128)(2,1)} %param.14) | copy-start | bytes 393220
  222.6 9.0 %collective-permute-start = (f32[32,8192]{1,0:T(8,128)}, f32[32,8192]{1,0:T(8,128)S(1)}, u32[]{:S(2)}, u32[]{:S(2)}) collective-permute-start(f32[32,8192]{1,0:T(8,128)} %slice_select_fusion), channel_id=1, source_target_pairs={{0,4},{4,0},{8,12},{12,8},{16,20},{20,16},{24,28},{28,24},{32,36},... | collective-permute-start | bytes 3145736 | tf_op jit(solution)/shard_map/ppermute | solution.py:14
  226.8 2.1 collective-permute-start.1
  229.0 2.7 collective-permute-start.3
  231.6 1.0 copy-start.2
  234.1 16.1 %collective-permute-start.2 = (f32[32,4096]{1,0:T(8,128)S(1)}, f32[32,4096]{1,0:T(8,128)S(1)}, u32[]{:S(2)}, u32[]{:S(2)}) collective-permute-start(f32[32,4096]{1,0:T(8,128)S(1)} %slice_select_fusion.1), channel_id=1, source_target_pairs={{0,8},{8,0},{4,12},{12,4},{16,24},{24,16},{20,28},{28,20},{32,40},... | collective-permute-start | bytes 1572872 | tf_op jit(solution)/shard_map/ppermute | solution.py:14
  234.4 10.0 %collective-permute-start.5 = (f32[2048]{0:T(1024)S(1)}, f32[2048]{0:T(1024)S(1)}, u32[]{:S(2)}, u32[]{:S(2)}) collective-permute-start(f32[2048]{0:T(1024)S(1)} %slice_select_fusion.8), channel_id=1, source_target_pairs={{0,16},{16,0},{4,20},{20,4},{8,24},{24,8},{12,28},{28,12},{32,48},... | collective-permute-start | bytes 24584 | tf_op jit(solution)/shard_map/ppermute | solution.py:14
  244.5 8.8 %collective-permute-start.7 = (f32[1024]{0:T(1024)S(1)}, f32[1024]{0:T(1024)S(1)}, u32[]{:S(2)}, u32[]{:S(2)}) collective-permute-start(f32[1024]{0:T(1024)S(1)} %slice_select_fusion.10), channel_id=1, source_target_pairs={{0,32},{32,0},{4,36},{36,4},{8,40},{40,8},{12,44},{44,12},{16,48},... | collective-permute-start | bytes 12296 | tf_op jit(solution)/shard_map/ppermute | solution.py:14
  250.3 13.8 %collective-permute-start.4 = (f32[32,2048]{1,0:T(8,128)S(1)}, f32[32,2048]{1,0:T(8,128)S(1)}, u32[]{:S(2)}, u32[]{:S(2)}) collective-permute-start(f32[32,2048]{1,0:T(8,128)S(1)} %slice_select_fusion.2), channel_id=1, source_target_pairs={{0,16},{16,0},{4,20},{20,4},{8,24},{24,8},{12,28},{28,12},{32,48},... | collective-permute-start | bytes 786440 | tf_op jit(solution)/shard_map/ppermute | solution.py:14
  253.2 12.5 %collective-permute-start.9 = (f32[512]{0:T(512)S(1)}, f32[512]{0:T(512)S(1)}, u32[]{:S(2)}, u32[]{:S(2)}) collective-permute-start(f32[512]{0:T(512)S(1)} %slice_select_fusion.12), channel_id=1, source_target_pairs={{0,64},{64,0},{4,68},{68,4},{8,72},{72,8},{12,76},{76,12},{16,80},... | collective-permute-start | bytes 6152 | tf_op jit(solution)/shard_map/ppermute | solution.py:14
  264.2 8.7 %collective-permute-start.6 = (f32[32,1024]{1,0:T(8,128)S(1)}, f32[32,1024]{1,0:T(8,128)S(1)}, u32[]{:S(2)}, u32[]{:S(2)}) collective-permute-start(f32[32,1024]{1,0:T(8,128)S(1)} %slice_select_fusion.3), channel_id=1, source_target_pairs={{0,32},{32,0},{4,36},{36,4},{8,40},{40,8},{12,44},{44,12},{16,48},... | collective-permute-start | bytes 393224 | tf_op jit(solution)/shard_map/ppermute | solution.py:14
  272.9 3.8 %collective-permute-start.8 = (f32[32,512]{1,0:T(8,128)S(1)}, f32[32,512]{1,0:T(8,128)S(1)}, u32[]{:S(2)}, u32[]{:S(2)}) collective-permute-start(f32[32,512]{1,0:T(8,128)S(1)} %slice_select_fusion.4), channel_id=1, source_target_pairs={{0,64},{64,0},{4,68},{68,4},{8,72},{72,8},{12,76},{76,12},{16,80},... | collective-permute-start | bytes 196616 | tf_op jit(solution)/shard_map/ppermute | solution.py:14
  274.2 4.8 %collective-permute-start.11 = (f32[256]{0:T(256)S(1)}, f32[256]{0:T(256)S(1)}, u32[]{:S(2)}, u32[]{:S(2)}) collective-permute-start(f32[256]{0:T(256)S(1)} %broadcast_select_fusion.7), channel_id=1, source_target_pairs={{0,128},{128,0},{4,132},{132,4},{8,136},{136,8},{12,140},{140,12},... | collective-permute-start | bytes 3080 | tf_op jit(solution)/shard_map/ppermute | solution.py:14
  276.7 4.7 %collective-permute-start.10 = (f32[32,256]{1,0:T(8,128)S(1)}, f32[32,256]{1,0:T(8,128)S(1)}, u32[]{:S(2)}, u32[]{:S(2)}) collective-permute-start(f32[32,256]{1,0:T(8,128)S(1)} %slice_select_fusion.5), channel_id=1, source_target_pairs={{0,128},{128,0},{4,132},{132,4},{8,136},{136,8},{12,140},{140,12},... | collective-permute-start | bytes 98312 | tf_op jit(solution)/shard_map/ppermute | solution.py:14
where the time goes:
time: 286 us; the launch traced here: 282 us
  other arithmetic  129 us (45%)
  local copies, waits for them, and re-layouts  51.7 us (18%)
  matrix products  33 us (12%)
  waiting for transfers between devices  30.3 us (11%)
  starting transfers between devices  24.8 us (9%)
  blocking collectives  12.8 us (4%)
    reduce_sum x1, other arithmetic, shade(): slab_color = jnp.sum(feats * weights[None, :, :], axis=2)  93.2 us
    ppermute x12, waiting for transfers between devices, swapped(): return lax.ppermute(block, axis, route)  30.3 us
    ppermute x12, starting transfers between devices, swapped(): return lax.ppermute(block, axis, route)  24.8 us
    slice x2, local copies, waits for them, and re-layouts, shade(): feats = field[:nfeat]  14.9 us
    dot_general x1, matrix products, shards(): jnp.einsum('hf,hs->fs', w_out, second, preferred_element_type=jnp.float32)  14.2 us
    all_gather x1, blocking collectives, shards(): table = lax.all_gather(bricks[0], 'ray', axis=0, tiled=True)  12.8 us
    dot_general x1, matrix products, shards(): jnp.einsum('ch,cs->hs', w_first, feats, preferred_element_type=jnp.float32)  12.5 us
    another operation x1, other arithmetic, shade(): before = jnp.cumsum(tau, axis=1) - tau  10.5 us
  transfers between devices with their start and end apart: 12, of which 6 were waited for; matrix products, arithmetic and copies ran while one was open for 0% of the time, Pallas kernels for 0%

commit v1 on v0

v1 whole, which is shorter than its diff:
```python
import functools

import jax
import jax.numpy as jnp
from jax import lax
from jax.experimental import pallas as pl
from jax.experimental.pallas import tpu as pltpu
from jax.sharding import PartitionSpec as P

BF = jnp.bfloat16
F32 = jnp.float32
MESH = pl.DeviceIdType.MESH

NX, NZ, NY = 4, 8, 4
TILES = 64
RAYS = 256
LANES = 128
GROUP = 4
STEPS = TILES // GROUP
ROWS = 72
USED = 66
CHUNKS = 8


def softplus(x):
    return jnp.maximum(x, 0.0) + jnp.log1p(jnp.exp(-jnp.abs(x)))


def put(ref, color, light):
    ref[0:32, :] = color[:, :LANES]
    ref[32:64, :] = color[:, LANES:]
    ref[64:65, :] = light[:, :LANES]
    ref[65:66, :] = light[:, LANES:]


def get(ref):
    return ref[0:32, :], ref[32:64, :], ref[64:65, :], ref[65:66, :]


def ordered(pieces):
    left, right, tleft, tright = pieces[0]
    for a, b, ta, tb in pieces[1:]:
        left = left + tleft * a
        right = right + tright * b
        tleft = tleft * ta
        tright = tright * tb
    return left, right, tleft, tright


def put4(ref, piece):
    ref[0:32, :] = piece[0]
    ref[32:64, :] = piece[1]
    ref[64:65, :] = piece[2]
    ref[65:66, :] = piece[3]


def kernel(
    bricks, index_hbm, interp, step_hbm, count_hbm, w1_hbm, w2_hbm, wo_hbm,
    color_out, light_out,
    table_bf, index, wv, step, count, w1, w2, wo, w2t,
    stage, table, h1a, h1b, h2a, h2b,
    mine, csend, crecv, zsend, zrecv, xsend, xrecv,
    in_sem, wv_sem, ysend_sem, yrecv_sem, cs_sem, cr_sem, zs_sem, zr_sem, xs_sem, xr_sem,
):
    region = lax.axis_index("region")
    y = lax.axis_index("ray")
    core = lax.rem(region, 2)
    z = lax.rem(region // 2, NZ)
    x = region // (2 * NZ)

    def at(px, pz, pc):
        return {"region": px * (2 * NZ) + pz * 2 + pc}

    small = [
        pltpu.make_async_copy(src, dst, in_sem.at[i])
        for i, (src, dst) in enumerate(
            [
                (w1_hbm, w1), (w2_hbm, w2), (wo_hbm, wo), (index_hbm.at[0], index),
                (step_hbm.at[0], step), (count_hbm, count),
                (bricks.at[0], table_bf.at[pl.ds(y * 128, 128)]),
            ]
        )
    ]
    for copy in small:
        copy.start()

    def wv_copy(c):
        n = TILES // CHUNKS
        return pltpu.make_async_copy(interp.at[0, pl.ds(c * n, n)], wv.at[pl.ds(c * n, n)], wv_sem.at[c])

    for c in range(CHUNKS):
        wv_copy(c).start()

    barrier = pltpu.get_barrier_semaphore()

    def hello(device):
        pl.semaphore_signal(barrier, inc=1, device_id=device, device_id_type=MESH)

    for d in range(1, NY):
        hello({"ray": lax.rem(y + d, NY)})
    hello(at(x, z, 1 - core))
    for d in range(1, NZ):
        hello(at(x, lax.rem(z + d, NZ), core))
    for d in range(1, NX):
        hello(at(lax.rem(x + d, NX), z, core))
    pl.semaphore_wait(barrier, (NY - 1) + 1 + (NZ - 1) + (NX - 1))

    def y_copy(d):
        return pltpu.make_async_remote_copy(
            src_ref=bricks.at[0],
            dst_ref=table_bf.at[pl.ds(y * 128, 128)],
            send_sem=ysend_sem.at[d],
            recv_sem=yrecv_sem.at[d],
            device_id={"ray": lax.rem(y + d, NY)},
            device_id_type=MESH,
        )

    for d in (1, 3, 2):
        y_copy(d).start()

    for copy in small:
        copy.wait()
    w2t[...] = w2[...].astype(F32).T.astype(BF)

    for c in range(CHUNKS):
        wv_copy(c).wait()

        @pl.loop(0, TILES // CHUNKS)
        def _(i):
            t = c * (TILES // CHUNKS) + i
            b = lax.rem(i, 2)
            stage[b] = wv[t].astype(F32)
            wv[t, 0:RAYS] = stage[b, pl.ds(0, RAYS, stride=2), :].astype(BF)
            wv[t, RAYS : 2 * RAYS] = stage[b, pl.ds(1, RAYS, stride=2), :].astype(BF)

    for d in range(1, NY):
        y_copy(d).wait()

    half = w1[...]
    none = jnp.zeros_like(half)
    wide = [jnp.concatenate([half, none], 0), jnp.concatenate([none, half], 0)]
    for v in range(8):
        cols = (v // 2) * LANES
        got = jnp.dot(table_bf[:, cols : cols + LANES], wide[v % 2], preferred_element_type=F32)
        flat = table.reshape(2, 4096, LANES)
        flat[0, pl.ds(v, 512, stride=8), :] = got[:, :LANES]
        flat[1, pl.ds(v, 512, stride=8), :] = got[:, LANES:]

    def offsets(i):
        j = lax.rem(i, 4)
        return 4 + j, 3 - j

    def column(k):
        return lax.rem(x + 1 + k, NX)

    def tile(i, u):
        off = offsets(i)[u % 2]
        c = core if u < 2 else 1 - core
        return column(i // 4) * (2 * NZ) + lax.rem(z + off, NZ) * 2 + c

    def layer1(i, h1):
        for u in range(GROUP):
            t = tile(i, u)
            ids = [index[j, t] for j in range(16)]
            g = [jnp.concatenate([table[h, b] for b in ids], 0).T for h in range(2)]
            g = jnp.concatenate(g, 0).astype(BF)
            r = lax.dot_general(g, wv[t], (((1,), (1,)), ((), ())), preferred_element_type=F32)
            h1[u * 256 : (u + 1) * 256] = jnp.maximum(r.astype(BF), 0)

    def layer2(h1, h2):
        for u in range(GROUP):
            r = jnp.dot(w2t[...], h1[u * 256 : (u + 1) * 256], preferred_element_type=F32)
            h2[u * 256 : (u + 1) * 256] = jnp.maximum(r.astype(BF), 0)

    def layer3(i, h2):
        for u in range(GROUP):
            t = tile(i, u)
            o = jnp.dot(wo[...], h2[u * 256 : (u + 1) * 256], preferred_element_type=F32)
            lanes = pl.ds(pl.multiple_of(t * RAYS, RAYS), RAYS)
            n = count[0:1, lanes]
            tau0 = softplus(o[32:33, :RAYS]) * step[0:1, lanes] * jnp.where(n > 0, 1.0, 0.0)
            tau1 = softplus(o[32:33, RAYS:]) * step[1:2, lanes] * jnp.where(n > 1, 1.0, 0.0)
            a0 = jnp.exp(-tau0)
            a1 = jnp.exp(-tau1)
            color = o[0:32, :RAYS] * (1.0 - a0) + o[0:32, RAYS:] * (a0 * (1.0 - a1))
            put((mine if u < 2 else csend).at[i, u % 2], color, a0 * a1)

    def c_copy(g):
        return pltpu.make_async_remote_copy(
            src_ref=csend.at[g],
            dst_ref=crecv.at[g],
            send_sem=cs_sem.at[g],
            recv_sem=cr_sem.at[g],
            device_id=at(x, z, 1 - core),
            device_id_type=MESH,
        )

    def z_copy(k, off):
        return pltpu.make_async_remote_copy(
            src_ref=zsend.at[k, off, pl.ds(0, USED)],
            dst_ref=zrecv.at[k, z, pl.ds(0, USED)],
            send_sem=zs_sem.at[k, off],
            recv_sem=zr_sem.at[k, z],
            device_id=at(x, lax.rem(z + off, NZ), core),
            device_id_type=MESH,
        )

    def z_wait(k, src):
        pltpu.make_async_copy(
            zrecv.at[k, src, pl.ds(0, USED)], zrecv.at[k, src, pl.ds(0, USED)], zr_sem.at[k, src]
        ).wait()

    def x_copy(k):
        return pltpu.make_async_remote_copy(
            src_ref=xsend.at[k, pl.ds(0, USED)],
            dst_ref=xrecv.at[x, pl.ds(0, USED)],
            send_sem=xs_sem.at[k],
            recv_sem=xr_sem.at[x],
            device_id=at(column(k), z, core),
            device_id_type=MESH,
        )

    def merge_cores(g):
        c_copy(g).wait_recv()
        front = core == 0
        k = g // 4
        off = offsets(g)
        for u in range(2):
            a, b = get(mine.at[g, u]), get(crecv.at[g, u])
            near = [jnp.where(front, p, q) for p, q in zip(a, b)]
            far = [jnp.where(front, q, p) for p, q in zip(a, b)]
            piece = ordered([near, far])
            if u == 0:
                put4(zsend.at[k, off[0]], piece)
                z_copy(k, off[0]).start()
            else:
                own = lax.rem(g, 4) == 3

                @pl.when(own)
                def _():
                    put4(zrecv.at[k, z], piece)

                @pl.when(jnp.logical_not(own))
                def _():
                    put4(zsend.at[k, off[1]], piece)
                    z_copy(k, off[1]).start()

    def merge_z(k):
        @pl.loop(1, NZ)
        def _(d):
            z_wait(k, lax.rem(z + d, NZ))

        return ordered([get(zrecv.at[k, s]) for s in range(NZ)])

    def hand_on(k):
        put4(xsend.at[k], merge_z(k))
        x_copy(k).start()

    def finish(i, h2):
        layer3(i, h2)
        c_copy(i).start()

    def work(i, now, before):
        layer3(i - 2, now[1])
        layer2(before[0], before[1])
        layer1(i, now[0])
        c_copy(i - 2).start()

        @pl.when(i >= 4)
        def _():
            merge_cores(i - 4)

        @pl.when(jnp.logical_and(i >= 11, lax.rem(i, 4) == 3))
        def _():
            hand_on((i - 11) // 4)

    even, odd = (h1a, h2a), (h1b, h2b)
    layer1(0, h1a)
    layer2(h1a, h2a)
    layer1(1, h1b)

    @pl.loop(1, STEPS // 2)
    def _(n):
        work(2 * n, even, odd)
        work(2 * n + 1, odd, even)

    layer3(STEPS - 2, h2a)
    layer2(h1b, h2b)
    c_copy(STEPS - 2).start()
    layer3(STEPS - 1, h2b)
    c_copy(STEPS - 1).start()

    @pl.loop(STEPS - 4, STEPS)
    def _(g):
        merge_cores(g)

    hand_on(2)
    put4(xrecv.at[x], merge_z(3))
    for d in range(1, NX):
        src = lax.rem(x + d, NX)
        pltpu.make_async_copy(xrecv.at[src, pl.ds(0, USED)], xrecv.at[src, pl.ds(0, USED)], xr_sem.at[src]).wait()
    left, right, tleft, tright = ordered([get(xrecv.at[s]) for s in range(NX)])
    color_out[:, :LANES] = left
    color_out[:, LANES:] = right
    light_out[:, :LANES] = tleft
    light_out[:, LANES:] = tright

    @pl.loop(0, STEPS)
    def _(g):
        c_copy(g).wait_send()
        z_copy(g // 4, offsets(g)[0]).wait_send()

        @pl.when(lax.rem(g, 4) < 3)
        def _():
            z_copy(g // 4, offsets(g)[1]).wait_send()

    for k in range(3):
        x_copy(k).wait_send()


def shards(bricks, pair_index, interp_weight, step_len, sample_count, w_first, w_second, w_out):
    part = functools.partial(pltpu.VMEM, dtype=F32)
    dma = pltpu.SemaphoreType.DMA
    color, light = pl.pallas_call(
        kernel,
        out_shape=(jax.ShapeDtypeStruct((32, RAYS), F32), jax.ShapeDtypeStruct((1, RAYS), F32)),
        in_specs=[pl.BlockSpec(memory_space=pl.ANY)] * 8,
        out_specs=[pl.BlockSpec(memory_space=pltpu.VMEM)] * 2,
        scratch_shapes=[
            pltpu.VMEM((512, 512), BF),
            pltpu.SMEM((16, 64), jnp.int32),
            pltpu.VMEM((TILES, 2 * RAYS, LANES), BF),
            pltpu.VMEM((2, TILES * RAYS), F32),
            pltpu.VMEM((1, TILES * RAYS), jnp.int32),
            pltpu.VMEM((64, 256), BF),
            pltpu.VMEM((256, 256), BF),
            pltpu.VMEM((33, 256), BF),
            pltpu.VMEM((256, 256), BF),
            pltpu.VMEM((2, 2 * RAYS, LANES), F32),
            pltpu.VMEM((2, 512, 8, LANES), F32),
        ]
        + [pltpu.VMEM((GROUP * 256, 512), BF)] * 4
        + [part((STEPS, 2, ROWS, LANES))] * 3
        + [part((NX, NZ, ROWS, LANES))] * 2
        + [part((NX, ROWS, LANES))] * 2
        + [dma((7,)), dma((CHUNKS,)), dma((NY,)), dma((NY,)), dma((STEPS,)), dma((STEPS,))]
        + [dma((NX, NZ)), dma((NX, NZ)), dma((NX,)), dma((NX,))],
        compiler_params=pltpu.CompilerParams(
            collective_id=0, has_side_effects=True, vmem_limit_bytes=50 * 2**20
        ),
        name="render",
    )(
        bricks,
        jnp.swapaxes(pair_index, 1, 2),
        interp_weight,
        step_len,
        sample_count,
        w_first,
        w_second,
        w_out.T,
    )
    return color, light.reshape(RAYS)


def solution(mesh):
    return jax.shard_map(
        shards,
        mesh=mesh,
        in_specs=(
            P("region", "ray", None),
            P("region", "ray", None),
            P("region", "ray", None, None),
            P("region", None, "ray"),
            P("region", "ray"),
            P(),
            P(),
            P(),
        ),
        out_specs=(P(None, ("ray", "region")), P(("ray", "region"))),
        check_vma=False,
    )
```

time: 286 us -> 57.1 us (0.20); the launches traced: 282 us -> 56.7 us
  other arithmetic: 129 us -> 0 us
  Pallas kernels: 0 us -> 49.2 us
  local copies, waits for them, and re-layouts: 51.7 us -> 6.9 us
  matrix products: 33 us -> 0 us
  waiting for transfers between devices: 30.3 us -> 0 us
  starting transfers between devices: 24.8 us -> 0 us
  blocking collectives: 12.8 us -> 0 us
    reduce_sum x2 -> x0, other arithmetic: 104 us -> none  [the longest x1 93.2 us: shade(): slab_color = jnp.sum(feats * weights[None, :, :], axis=2)]
    pallas_call x0 -> x1, Pallas kernels: none -> 49.2 us  [shards(): pl.pallas_call(kernel, out_shape=(jax.ShapeDtypeStruct((32, RAYS), F32),...]
    dot_general x3 -> x0, matrix products: 33 us -> none  [the longest x1 14.2 us: shards(): jnp.einsum('hf,hs->fs', w_out, second, preferred_element_type=jnp.float32)]
    ppermute x12 -> x0, waiting for transfers between devices: 30.3 us -> none  [swapped(): return lax.ppermute(block, axis, route)]
    ppermute x12 -> x0, starting transfers between devices: 24.8 us -> none  [swapped(): return lax.ppermute(block, axis, route)]
    slice x3 -> x0, local copies, waits for them, and re-layouts: 16.4 us -> none  [the longest x2 14.9 us: shade(): feats = field[:nfeat]]
    all_gather x1 -> x0, blocking collectives: 12.8 us -> none  [shards(): table = lax.all_gather(bricks[0], 'ray', axis=0, tiled=True)]
    another operation x1 -> x0, other arithmetic: 10.5 us -> none  [shade(): before = jnp.cumsum(tau, axis=1) - tau]
  transfers between devices with their start and end apart: 12 -> 0, of which waited for: 6 -> 0; matrix products, arithmetic and copies ran while one was open for 0% -> 0% of each run, Pallas kernels for 0% -> 0%
where the time goes in v1:
time: 57.1 us; the launch traced here: 56.7 us
  Pallas kernels  49.2 us (86%)
  local copies, waits for them, and re-layouts  6.9 us (12%)
  between operations  0.66 us (1%)
    pallas_call x1, Pallas kernels, shards(): pl.pallas_call(kernel, out_shape=(jax.ShapeDtypeStruct((32, RAYS), F32),...  49.2 us
    unnamed x16, local copies, waits for them, and re-layouts  6.9 us

profile of v1, /device:TPU:1, one launch (start us, length us, event | category | flops | bytes accessed | tf_op | source)
XLA Modules:
  0.0 56.7 jit_solution(7386743879984983341)
XLA Ops:
  0.6 0.0 copy-start
  0.6 0.9 %copy-done = bf16[1,128,512]{2,1,0:T(8,128)(2,1)S(1)} copy-done((bf16[1,128,512]{2,1,0:T(8,128)(2,1)S(1)}, bf16[1,128,512]{2,1,0:T(8,128)(2,1)}, u32[]{:S(2)}) %copy-start) | copy-done | bytes 131096
  1.5 0.0 copy-start.1
  1.5 0.9 %copy-done.1 = f32[1,2,16384]{2,1,0:T(2,128)S(1)} copy-done((f32[1,2,16384]{2,1,0:T(2,128)S(1)}, f32[1,2,16384]{2,1,0:T(2,128)}, u32[]{:S(2)}) %copy-start.1) | copy-done | bytes 131096
  2.4 0.0 copy-start.2
  2.4 0.9 %copy-done.2 = bf16[256,256]{1,0:T(8,128)(2,1)S(1)} copy-done((bf16[256,256]{1,0:T(8,128)(2,1)S(1)}, bf16[256,256]{1,0:T(8,128)(2,1)}, u32[]{:S(2)}) %copy-start.2) | copy-done | bytes 131096
  3.3 0.0 copy-start.3
  3.3 0.8 %copy-done.3 = s32[1,16384]{1,0:T(1,128)S(1)} copy-done((s32[1,16384]{1,0:T(1,128)S(1)}, s32[1,16384]{1,0:T(1,128)}, u32[]{:S(2)}) %copy-start.3) | copy-done | bytes 65560
  4.2 0.0 copy-start.4
  4.2 0.8 %copy-done.4 = bf16[64,256]{1,0:T(8,128)(2,1)S(1)} copy-done((bf16[64,256]{1,0:T(8,128)(2,1)S(1)}, bf16[64,256]{1,0:T(8,128)(2,1)}, u32[]{:S(2)}) %copy-start.4) | copy-done | bytes 32792
  4.9 0.0 copy-start.5
  4.9 0.7 %copy-done.5 = bf16[256,33]{0,1:T(8,128)(2,1)S(1)} copy-done((bf16[256,33]{0,1:T(8,128)(2,1)S(1)}, bf16[256,33]{0,1:T(8,128)(2,1)}, u32[]{:S(2)}) %copy-start.5) | copy-done | bytes 16920
  5.7 0.0 copy-start.6
  5.7 0.7 %copy-done.6 = s32[1,64,16]{1,2,0:T(8,128)S(1)} copy-done((s32[1,64,16]{1,2,0:T(8,128)S(1)}, s32[1,64,16]{1,2,0:T(8,128)}, u32[]{:S(2)}) %copy-start.6) | copy-done | bytes 4120
  6.4 49.2 %render.1 = (f32[32,256]{1,0:T(8,128)S(1)}, f32[1,256]{1,0:T(1,128)S(1)}) custom-call(bf16[1,128,512]{2,1,0:T(8,128)(2,1)S(1)} %copy-done, s32[1,16,64]{2,1,0:T(8,128)S(1)} %bitcast.4, bf16[1,64,512,128]{3,2,1,0:T(8,128)(2,1)} %interp.1, f32[1,2,16384]{2,1,0:T(2,128)S(1)} %copy-done.1, s32[1,16384]{1,0:T(1,128)S(1)} %copy-done.3, ...), custom_call_target="tpu_custom_call" | custom-call | tf_op jit(solution)/shard_map/render/pallas_call | solution.py:324
  55.6 0.6 %copy.12 = f32[32,256]{1,0:T(8,128)} copy(f32[32,256]{1,0:T(8,128)S(1)} %get-tuple-element.8) | data formatting | bytes 65536
  56.2 0.6 copy.13
Async XLA Ops:
  0.6 0.9 %copy-start = (bf16[1,128,512]{2,1,0:T(8,128)(2,1)S(1)}, bf16[1,128,512]{2,1,0:T(8,128)(2,1)}, u32[]{:S(2)}) copy-start(bf16[1,128,512]{2,1,0:T(8,128)(2,1)} %bricks.1) | copy-start | bytes 393220
  1.5 0.9 %copy-start.1 = (f32[1,2,16384]{2,1,0:T(2,128)S(1)}, f32[1,2,16384]{2,1,0:T(2,128)}, u32[]{:S(2)}) copy-start(f32[1,2,16384]{2,1,0:T(2,128)} %step_hbm.1) | copy-start | bytes 393220
  2.4 0.9 %copy-start.2 = (bf16[256,256]{1,0:T(8,128)(2,1)S(1)}, bf16[256,256]{1,0:T(8,128)(2,1)}, u32[]{:S(2)}) copy-start(bf16[256,256]{1,0:T(8,128)(2,1)} %w2_hbm.1) | copy-start | bytes 393220
  3.3 0.8 %copy-start.3 = (s32[1,16384]{1,0:T(1,128)S(1)}, s32[1,16384]{1,0:T(1,128)}, u32[]{:S(2)}) copy-start(s32[1,16384]{1,0:T(1,128)} %count_hbm.1) | copy-start | bytes 196612
  4.2 0.8 %copy-start.4 = (bf16[64,256]{1,0:T(8,128)(2,1)S(1)}, bf16[64,256]{1,0:T(8,128)(2,1)}, u32[]{:S(2)}) copy-start(bf16[64,256]{1,0:T(8,128)(2,1)} %w1_hbm.1) | copy-start | bytes 98308
  4.9 0.7 %copy-start.5 = (bf16[256,33]{0,1:T(8,128)(2,1)S(1)}, bf16[256,33]{0,1:T(8,128)(2,1)}, u32[]{:S(2)}) copy-start(bf16[256,33]{0,1:T(8,128)(2,1)} %param.15) | copy-start | bytes 50692
  5.7 0.7 %copy-start.6 = (s32[1,64,16]{1,2,0:T(8,128)S(1)}, s32[1,64,16]{1,2,0:T(8,128)}, u32[]{:S(2)}) copy-start(s32[1,64,16]{1,2,0:T(8,128)} %param.9) | copy-start | bytes 12292

commit v2 on v1

--- a/solution.py
+++ b/solution.py
@@ -20,6 +20,8 @@
 ROWS = 72
 USED = 66
 CHUNKS = 8
+FORWARD = 3
+TOP = 32700.0
 
 
 def softplus(x):
@@ -59,7 +61,7 @@
     color_out, light_out,
     table_bf, index, wv, step, count, w1, w2, wo, w2t,
     stage, table, h1a, h1b, h2a, h2b,
-    mine, csend, crecv, zsend, zrecv, xsend, xrecv,
+    mine, csend, crecv, zsend, zrecv, zmsend, zmrecv, xsend, xrecv,
     in_sem, wv_sem, ysend_sem, yrecv_sem, cs_sem, cr_sem, zs_sem, zr_sem, xs_sem, xr_sem,
 ):
     region = lax.axis_index("region")
@@ -71,6 +73,18 @@
     def at(px, pz, pc):
         return {"region": px * (2 * NZ) + pz * 2 + pc}
 
+    barrier = pltpu.get_barrier_semaphore()
+
+    def hello(device):
+        pl.semaphore_signal(barrier, inc=1, device_id=device, device_id_type=MESH)
+
+    for d in range(1, NY):
+        hello({"ray": lax.rem(y + d, NY)})
+    hello(at(x, z, 1 - core))
+    for d in range(1, NZ):
+        hello(at(x, lax.rem(z + d, NZ), core))
+    for d in range(1, NX):
+        hello(at(lax.rem(x + d, NX), z, core))
     small = [
         pltpu.make_async_copy(src, dst, in_sem.at[i])
         for i, (src, dst) in enumerate(
@@ -91,38 +105,34 @@
     for c in range(CHUNKS):
         wv_copy(c).start()
 
-    barrier = pltpu.get_barrier_semaphore()
-
-    def hello(device):
-        pl.semaphore_signal(barrier, inc=1, device_id=device, device_id_type=MESH)
-
-    for d in range(1, NY):
-        hello({"ray": lax.rem(y + d, NY)})
-    hello(at(x, z, 1 - core))
-    for d in range(1, NZ):
-        hello(at(x, lax.rem(z + d, NZ), core))
-    for d in range(1, NX):
-        hello(at(lax.rem(x + d, NX), z, core))
     pl.semaphore_wait(barrier, (NY - 1) + 1 + (NZ - 1) + (NX - 1))
 
-    def y_copy(d):
+    def half_of(owner, h):
+        return table_bf.at[pl.ds(lax.rem(owner + NY, NY) * 128 + h * 64, 64)]
+
+    def y_copy(n):
+        owner, h, to = ((y, 0, 1), (y, 1, 3), (y, 1, 1), (y, 0, 3), (y - 1, 0, 1), (y + 1, 1, 3))[n]
         return pltpu.make_async_remote_copy(
-            src_ref=bricks.at[0],
-            dst_ref=table_bf.at[pl.ds(y * 128, 128)],
-            send_sem=ysend_sem.at[d],
-            recv_sem=yrecv_sem.at[d],
-            device_id={"ray": lax.rem(y + d, NY)},
+            src_ref=half_of(owner, h) if n >= 4 else bricks.at[0, pl.ds(h * 64, 64)],
+            dst_ref=half_of(owner, h),
+            send_sem=ysend_sem.at[n],
+            recv_sem=yrecv_sem.at[n],
+            device_id={"ray": lax.rem(y + to, NY)},
             device_id_type=MESH,
         )
 
-    for d in (1, 3, 2):
-        y_copy(d).start()
+    for n in range(4):
+        y_copy(n).start()
 
     for copy in small:
         copy.wait()
     w2t[...] = w2[...].astype(F32).T.astype(BF)
 
     for c in range(CHUNKS):
+        if c == FORWARD:
+            for n in range(2):
+                y_copy(n).wait_recv()
+                y_copy(4 + n).start()
         wv_copy(c).wait()
 
         @pl.loop(0, TILES // CHUNKS)
@@ -133,8 +143,8 @@
             wv[t, 0:RAYS] = stage[b, pl.ds(0, RAYS, stride=2), :].astype(BF)
             wv[t, RAYS : 2 * RAYS] = stage[b, pl.ds(1, RAYS, stride=2), :].astype(BF)
 
-    for d in range(1, NY):
-        y_copy(d).wait()
+    for n in range(2, 6):
+        y_copy(n).wait_recv()
 
     half = w1[...]
     none = jnp.zeros_like(half)
@@ -195,20 +205,40 @@
             device_id_type=MESH,
         )
 
-    def z_copy(k, off):
-        return pltpu.make_async_remote_copy(
-            src_ref=zsend.at[k, off, pl.ds(0, USED)],
-            dst_ref=zrecv.at[k, z, pl.ds(0, USED)],
-            send_sem=zs_sem.at[k, off],
-            recv_sem=zr_sem.at[k, z],
-            device_id=at(x, lax.rem(z + off, NZ), core),
-            device_id_type=MESH,
-        )
+    def z_copies(k, off):
+        to = at(x, lax.rem(z + off, NZ), core)
+        return [
+            pltpu.make_async_remote_copy(
+                src_ref=src.at[k, off, pl.ds(0, n)],
+                dst_ref=dst.at[k, z, pl.ds(0, n)],
+                send_sem=zs_sem.at[h, k, off],
+                recv_sem=zr_sem.at[h, k, z],
+                device_id=to,
+                device_id_type=MESH,
+            )
+            for h, (src, dst, n) in enumerate([(zsend, zrecv, 64), (zmsend, zmrecv, 4)])
+        ]
 
     def z_wait(k, src):
-        pltpu.make_async_copy(
-            zrecv.at[k, src, pl.ds(0, USED)], zrecv.at[k, src, pl.ds(0, USED)], zr_sem.at[k, src]
-        ).wait()
+        for h, (ref, n) in enumerate([(zrecv, 64), (zmrecv, 4)]):
+            got = ref.at[k, src, pl.ds(0, n)]
+            pltpu.make_async_copy(got, got, zr_sem.at[h, k, src]).wait()
+
+    def code(colors, lights, piece):
+        for h in range(2):
+            most = jnp.max(jnp.abs(piece[h]), axis=0, keepdims=True)
+            colors[32 * h : 32 * h + 32, :] = (
+                (piece[h] * (TOP / jnp.maximum(most, 1e-30))).astype(jnp.int32).astype(jnp.int16)
+            )
+            lights[h : h + 1, :] = piece[2 + h]
+            lights[2 + h : 3 + h, :] = jnp.maximum(most, 1e-30) * (1.0 / TOP)
+
+    def decode(colors, lights):
+        halves = [
+            colors[32 * h : 32 * h + 32, :].astype(jnp.int32).astype(F32) * lights[2 + h : 3 + h, :]
+            for h in range(2)
+        ]
+        return halves[0], halves[1], lights[0:1, :], lights[1:2, :]
 
     def x_copy(k):
         return pltpu.make_async_remote_copy(
@@ -231,26 +261,28 @@
             far = [jnp.where(front, q, p) for p, q in zip(a, b)]
             piece = ordered([near, far])
             if u == 0:
-                put4(zsend.at[k, off[0]], piece)
-                z_copy(k, off[0]).start()
+                code(zsend.at[k, off[0]], zmsend.at[k, off[0]], piece)
+                for copy in z_copies(k, off[0]):
+                    copy.start()
             else:
                 own = lax.rem(g, 4) == 3
 
                 @pl.when(own)
                 def _():
-                    put4(zrecv.at[k, z], piece)
+                    code(zrecv.at[k, z], zmrecv.at[k, z], piece)
 
                 @pl.when(jnp.logical_not(own))
                 def _():
-                    put4(zsend.at[k, off[1]], piece)
-                    z_copy(k, off[1]).start()
+                    code(zsend.at[k, off[1]], zmsend.at[k, off[1]], piece)
+                    for copy in z_copies(k, off[1]):
+                        copy.start()
 
     def merge_z(k):
         @pl.loop(1, NZ)
         def _(d):
             z_wait(k, lax.rem(z + d, NZ))
 
-        return ordered([get(zrecv.at[k, s]) for s in range(NZ)])
+        return ordered([decode(zrecv.at[k, s], zmrecv.at[k, s]) for s in range(NZ)])
 
     def hand_on(k):
         put4(xsend.at[k], merge_z(k))
@@ -305,14 +337,19 @@
     light_out[:, :LANES] = tleft
     light_out[:, LANES:] = tright
 
+    for n in range(6):
+        y_copy(n).wait_send()
+
     @pl.loop(0, STEPS)
     def _(g):
         c_copy(g).wait_send()
-        z_copy(g // 4, offsets(g)[0]).wait_send()
+        for copy in z_copies(g // 4, offsets(g)[0]):
+            copy.wait_send()
 
         @pl.when(lax.rem(g, 4) < 3)
         def _():
-            z_copy(g // 4, offsets(g)[1]).wait_send()
+            for copy in z_copies(g // 4, offsets(g)[1]):
+                copy.wait_send()
 
     for k in range(3):
         x_copy(k).wait_send()
@@ -324,7 +361,7 @@
     color, light = pl.pallas_call(
         kernel,
         out_shape=(jax.ShapeDtypeStruct((32, RAYS), F32), jax.ShapeDtypeStruct((1, RAYS), F32)),
-        in_specs=[pl.BlockSpec(memory_space=pl.ANY)] * 8,
+        in_specs=[pl.BlockSpec(memory_space=pltpu.HBM)] * 8,
         out_specs=[pl.BlockSpec(memory_space=pltpu.VMEM)] * 2,
         scratch_shapes=[
             pltpu.VMEM((512, 512), BF),
@@ -341,12 +378,13 @@
         ]
         + [pltpu.VMEM((GROUP * 256, 512), BF)] * 4
         + [part((STEPS, 2, ROWS, LANES))] * 3
-        + [part((NX, NZ, ROWS, LANES))] * 2
+        + [pltpu.VMEM((NX, NZ, 64, LANES), jnp.int16)] * 2
+        + [part((NX, NZ, 8, LANES))] * 2
         + [part((NX, ROWS, LANES))] * 2
-        + [dma((7,)), dma((CHUNKS,)), dma((NY,)), dma((NY,)), dma((STEPS,)), dma((STEPS,))]
-        + [dma((NX, NZ)), dma((NX, NZ)), dma((NX,)), dma((NX,))],
+        + [dma((7,)), dma((CHUNKS,)), dma((6,)), dma((6,)), dma((STEPS,)), dma((STEPS,))]
+        + [dma((2, NX, NZ)), dma((2, NX, NZ)), dma((NX,)), dma((NX,))],
         compiler_params=pltpu.CompilerParams(
-            collective_id=0, has_side_effects=True, vmem_limit_bytes=50 * 2**20
+            collective_id=0, has_side_effects=True, vmem_limit_bytes=62 * 2**20
         ),
         name="render",
     )(

time: 57.1 us -> 45.4 us (0.80)
  Pallas kernels: 49.2 us -> 42 us
  local copies, waits for them, and re-layouts: 6.9 us -> 2.6 us
    pallas_call x1, Pallas kernels: 49.2 us -> 42 us  [shards(): pl.pallas_call(kernel, out_shape=(jax.ShapeDtypeStruct((32, RAYS), F32),...]
    unnamed x16 -> x2, local copies, waits for them, and re-layouts: 6.9 us -> 2.6 us
where the time goes in v2:
time: 45.4 us; the launch traced here: 45.3 us
  Pallas kernels  42 us (93%)
  local copies, waits for them, and re-layouts  2.6 us (6%)
  between operations  0.64 us (1%)
    pallas_call x1, Pallas kernels, shards(): pl.pallas_call(kernel, out_shape=(jax.ShapeDtypeStruct((32, RAYS), F32),...  42 us
    unnamed x2, local copies, waits for them, and re-layouts  2.6 us

profile of v2, /device:TPU:1, one launch (start us, length us, event | category | flops | bytes accessed | tf_op | source)
XLA Modules:
  0.0 45.3 jit_solution(6107075700718185513)
XLA Ops:
  0.6 42.0 %render.1 = (f32[32,256]{1,0:T(8,128)}, f32[1,256]{1,0:T(1,128)}) custom-call(bf16[1,128,512]{2,1,0:T(8,128)(2,1)} %bricks.1, s32[1,16,64]{2,1,0:T(8,128)} %bitcast.4, bf16[1,64,512,128]{3,2,1,0:T(8,128)(2,1)} %interp.1, f32[1,2,16384]{2,1,0:T(2,128)} %step_hbm.1, s32[1,16384]{1,0:T(1,128)} %count_hbm.1, bf16[64,256]{1,0:T(8,128)(2,1)} %w1_hbm.1, ...), custom_call_target="tpu_custom_call" | custom-call | tf_op jit(solution)/shard_map/render/pallas_call | solution.py:361
  42.6 1.4 %copy.12 = f32[32,256]{1,0:T(8,128)} copy(f32[32,256]{1,0:T(8,128)} %get-tuple-element.8) | data formatting | bytes 65536
  44.0 1.2 %copy.13 = f32[256]{0:T(256)} copy(f32[256]{0:T(256)} %bitcast.5) | data formatting | bytes 2048

commit v3 on v2

v3 whole, which is shorter than its diff:
```python
import functools

import jax
import jax.numpy as jnp
from jax import lax
from jax.experimental import pallas as pl
from jax.experimental.pallas import tpu as pltpu
from jax.sharding import PartitionSpec as P

BF = jnp.bfloat16
F32 = jnp.float32
MESH = pl.DeviceIdType.MESH

NX, NZ, NY = 4, 8, 4
TILES = 64
RAYS = 256
LANES = 128
GROUP = 4
PAIRS = TILES // 4
LEAD = 4
STEPS = TILES // GROUP
ROWS = 72
USED = 66
CHUNKS = 8
FORWARD = 3
FINE = 2.0**20
TOP = 32700.0


def softplus(x):
    return jnp.maximum(x, 0.0) + jnp.log1p(jnp.exp(-jnp.abs(x)))


def put(ref, color, light):
    ref[0:32, :] = color[:, :LANES]
    ref[32:64, :] = color[:, LANES:]
    ref[64:65, :] = light[:, :LANES]
    ref[65:66, :] = light[:, LANES:]


def get(ref):
    return ref[0:32, :], ref[32:64, :], ref[64:65, :], ref[65:66, :]


def ordered(pieces):
    left, right, tleft, tright = pieces[0]
    for a, b, ta, tb in pieces[1:]:
        left = left + tleft * a
        right = right + tright * b
        tleft = tleft * ta
        tright = tright * tb
    return left, right, tleft, tright


def put4(ref, piece):
    ref[0:32, :] = piece[0]
    ref[32:64, :] = piece[1]
    ref[64:65, :] = piece[2]
    ref[65:66, :] = piece[3]


def kernel(
    bricks, index_hbm, interp, step_hbm, count_hbm, w1_hbm, w2_hbm, wo_hbm,
    color_out, light_out,
    table_bf, index, wv, step, count, w1, w2, wo, w2t,
    stage, table, h1a, h1b, h2a, h2b,
    csend, crecv, zsend, zrecv, xsend, xrecv,
    in_sem, wv_sem, ysend_sem, yrecv_sem, cs_sem, cr_sem, zs_sem, zr_sem, xs_sem, xr_sem,
):
    region = lax.axis_index("region")
    y = lax.axis_index("ray")
    core = lax.rem(region, 2)
    z = lax.rem(region // 2, NZ)
    x = region // (2 * NZ)

    def at(px, pz, pc):
        return {"region": px * (2 * NZ) + pz * 2 + pc}

    barrier = pltpu.get_barrier_semaphore()

    def hello(device):
        pl.semaphore_signal(barrier, inc=1, device_id=device, device_id_type=MESH)

    for d in range(1, NY):
        hello({"ray": lax.rem(y + d, NY)})
    hello(at(x, z, 1 - core))
    for d in range(1, NZ):
        hello(at(x, lax.rem(z + d, NZ), core))
    for d in range(1, NX):
        hello(at(lax.rem(x + d, NX), z, core))
    small = [
        pltpu.make_async_copy(src, dst, in_sem.at[i])
        for i, (src, dst) in enumerate(
            [
                (w1_hbm, w1), (w2_hbm, w2), (wo_hbm, wo), (index_hbm.at[0], index),
                (step_hbm.at[0], step), (count_hbm, count),
                (bricks.at[0], table_bf.at[pl.ds(y * 128, 128)]),
            ]
        )
    ]
    for copy in small:
        copy.start()

    def wv_copy(c):
        n = TILES // CHUNKS
        return pltpu.make_async_copy(interp.at[0, pl.ds(c * n, n)], wv.at[pl.ds(c * n, n)], wv_sem.at[c])

    for c in range(CHUNKS):
        wv_copy(c).start()

    pl.semaphore_wait(barrier, (NY - 1) + 1 + (NZ - 1) + (NX - 1))

    def half_of(owner, h):
        return table_bf.at[pl.ds(lax.rem(owner + NY, NY) * 128 + h * 64, 64)]

    def y_copy(n):
        owner, h, to = ((y, 0, 1), (y, 1, 3), (y, 1, 1), (y, 0, 3), (y - 1, 0, 1), (y + 1, 1, 3))[n]
        return pltpu.make_async_remote_copy(
            src_ref=half_of(owner, h) if n >= 4 else bricks.at[0, pl.ds(h * 64, 64)],
            dst_ref=half_of(owner, h),
            send_sem=ysend_sem,
            recv_sem=yrecv_sem.at[n],
            device_id={"ray": lax.rem(y + to, NY)},
            device_id_type=MESH,
        )

    for n in range(4):
        y_copy(n).start()

    for copy in small:
        copy.wait()
    w2t[...] = w2[...].astype(F32).T.astype(BF)

    for c in range(CHUNKS):
        if c == FORWARD:
            for n in range(2):
                y_copy(n).wait_recv()
                y_copy(4 + n).start()
        wv_copy(c).wait()

        @pl.loop(0, TILES // CHUNKS)
        def _(i):
            t = c * (TILES // CHUNKS) + i
            b = lax.rem(i, 2)
            stage[b] = wv[t].astype(F32)
            wv[t, 0:RAYS] = stage[b, pl.ds(0, RAYS, stride=2), :].astype(BF)
            wv[t, RAYS : 2 * RAYS] = stage[b, pl.ds(1, RAYS, stride=2), :].astype(BF)

    for n in range(2, 6):
        y_copy(n).wait_recv()

    half = w1[...]
    none = jnp.zeros_like(half)
    wide = [jnp.concatenate([half, none], 0), jnp.concatenate([none, half], 0)]
    for v in range(8):
        cols = (v // 2) * LANES
        got = jnp.dot(table_bf[:, cols : cols + LANES], wide[v % 2], preferred_element_type=F32)
        flat = table.reshape(2, 4096, LANES)
        flat[0, pl.ds(v, 512, stride=8), :] = got[:, :LANES]
        flat[1, pl.ds(v, 512, stride=8), :] = got[:, LANES:]

    def offsets(p):
        j = lax.rem(p, 4)
        return 4 + j, 3 - j

    def column(k):
        return lax.rem(x + 1 + k, NX)

    def tile(p, u, c):
        return column(p // 4) * (2 * NZ) + lax.rem(z + offsets(p)[u], NZ) * 2 + c

    def tiles(i):
        first, last = i < LEAD // 2, i >= STEPS - LEAD // 2
        a = jnp.where(first, 2 * i, jnp.where(last, 2 * i - PAIRS, i + LEAD // 2))
        b = jnp.where(first, 2 * i + 1, jnp.where(last, 2 * i - PAIRS + 1, i - LEAD // 2))
        ca = jnp.where(last, core, 1 - core)
        cb = jnp.where(first, 1 - core, core)
        return [tile(a, 0, ca), tile(a, 1, ca), tile(b, 0, cb), tile(b, 1, cb)]

    def layer1(i, h1):
        for u, t in enumerate(tiles(i)):
            ids = [index[j, t] for j in range(16)]
            g = [jnp.concatenate([table[h, b] for b in ids], 0).T for h in range(2)]
            g = jnp.concatenate(g, 0).astype(BF)
            r = lax.dot_general(g, wv[t], (((1,), (1,)), ((), ())), preferred_element_type=F32)
            h1[u * 256 : (u + 1) * 256] = jnp.maximum(r.astype(BF), 0)

    def layer2(h1, h2):
        for u in range(GROUP):
            r = jnp.dot(w2t[...], h1[u * 256 : (u + 1) * 256], preferred_element_type=F32)
            h2[u * 256 : (u + 1) * 256] = jnp.maximum(r.astype(BF), 0)

    def shade(h2, u, t):
        o = jnp.dot(wo[...], h2[u * 256 : (u + 1) * 256], preferred_element_type=F32)
        lanes = pl.ds(pl.multiple_of(t * RAYS, RAYS), RAYS)
        n = count[0:1, lanes]
        tau0 = softplus(o[32:33, :RAYS]) * step[0:1, lanes] * jnp.where(n > 0, 1.0, 0.0)
        tau1 = softplus(o[32:33, RAYS:]) * step[1:2, lanes] * jnp.where(n > 1, 1.0, 0.0)
        a0 = jnp.exp(-tau0)
        a1 = jnp.exp(-tau1)
        color = o[0:32, :RAYS] * (1.0 - a0) + o[0:32, RAYS:] * (a0 * (1.0 - a1))
        return color, a0 * a1

    def shade_other(p, h2, u):
        for v in range(2):
            put(csend.at[p, v], *shade(h2, u + v, tile(p, v, 1 - core)))

    def shade_own(p, h2, u):
        front = core == 0
        for v in range(2):
            color, light = shade(h2, u + v, tile(p, v, core))
            left, right, tleft, tright = get(crecv.at[p, v])
            piece = []
            for a, ta, b, tb in (
                (color[:, :LANES], light[:, :LANES], left, tleft),
                (color[:, LANES:], light[:, LANES:], right, tright),
            ):
                piece.append(a * jnp.where(front, 1.0, tb) + b * jnp.where(front, ta, 1.0))
                piece.append(ta * tb)
            off = offsets(p)[v]
            code(zsend.at[p // 4, off], piece[0::2] + piece[1::2])

    def c_copy(n):
        return pltpu.make_async_remote_copy(
            src_ref=csend.at[pl.ds(2 * n, 2)],
            dst_ref=crecv.at[pl.ds(2 * n, 2)],
            send_sem=cs_sem,
            recv_sem=cr_sem.at[n],
            device_id=at(x, z, 1 - core),
            device_id_type=MESH,
        )

    def wait_for(ref, sem):
        pltpu.make_async_copy(ref, ref, sem).wait()

    def z_copy(k, off):
        return pltpu.make_async_remote_copy(
            src_ref=zsend.at[k, off],
            dst_ref=zrecv.at[k, z],
            send_sem=zs_sem,
            recv_sem=zr_sem.at[k],
            device_id=at(x, lax.rem(z + off, NZ), core),
            device_id_type=MESH,
        )

    def code(ref, piece):
        row = lax.broadcasted_iota(jnp.int32, (16, LANES), 0)
        kind = jnp.bitwise_and(row, 3)
        top = []
        for h in range(2):
            most = jnp.maximum(jnp.max(jnp.abs(piece[h]), axis=0, keepdims=True), 1e-30)
            ref[32 * h : 32 * h + 32, :] = (piece[h] * (TOP / most)).astype(jnp.int32).astype(jnp.int16)
            top.append(most * (1.0 / TOP))
        value = jnp.where(
            kind < 2,
            jnp.where(kind == 0, piece[2], piece[3]),
            jnp.where(kind == 2, top[0], top[1]),
        )
        fixed = (jnp.log(jnp.maximum(value, 1e-37)) * FINE).astype(jnp.int32)
        parts = jnp.where(row < 4, jnp.right_shift(fixed, 15), jnp.bitwise_and(fixed, 32767))
        ref[64:80, :] = jnp.where(row < 8, parts, 0).astype(jnp.int16)

    def decode(ref):
        parts = ref[64:80, :].astype(jnp.int32)
        value = jnp.exp(parts[0:4].astype(F32) * (32768.0 / FINE) + parts[4:8].astype(F32) * (1.0 / FINE))
        halves = [
            ref[32 * h : 32 * h + 32, :].astype(jnp.int32).astype(F32) * value[2 + h : 3 + h] for h in range(2)
        ]
        return halves[0], halves[1], value[0:1], value[1:2]

    def x_copy(k):
        return pltpu.make_async_remote_copy(
            src_ref=xsend.at[k, pl.ds(0, USED)],
            dst_ref=xrecv.at[x, pl.ds(0, USED)],
            send_sem=xs_sem,
            recv_sem=xr_sem,
            device_id=at(column(k), z, core),
            device_id_type=MESH,
        )

    def send_own(p):
        k, off = p // 4, offsets(p)
        z_copy(k, off[0]).start()
        own = lax.rem(p, 4) == 3

        @pl.when(own)
        def _():
            zrecv[k, z] = zsend[k, 0]

        @pl.when(jnp.logical_not(own))
        def _():
            z_copy(k, off[1]).start()

    def merge_z(k):
        wait_for(zrecv.at[k, pl.ds(0, NZ - 1)], zr_sem.at[k])
        return ordered([decode(zrecv.at[k, s]) for s in range(NZ)])

    def hand_on(k):
        put4(xsend.at[k], merge_z(k))
        x_copy(k).start()

    def compute(i, now, before):
        layer2(before[0], before[1])
        layer1(i, now[0])

    def work(i, now, before):
        shade_other(i, now[1], 0)
        shade_own(i - 4, now[1], 2)
        compute(i, now, before)
        send_own(i - 4)

    even, odd = (h1a, h2a), (h1b, h2b)
    layer1(0, h1a)
    layer2(h1a, h2a)
    layer1(1, h1b)
    for i in range(2, 4):
        now, before = (even, odd) if i % 2 == 0 else (odd, even)
        first = 2 * (i - 2)
        for n in range(2):
            shade_other(first + n, now[1], 2 * n)
        compute(i, now, before)
        c_copy(i - 2).start()

    @pl.loop(2, STEPS // 2)
    def _(n):
        c_copy(n - 2).wait_recv()
        work(2 * n, even, odd)

        work(2 * n + 1, odd, even)
        c_copy(n).start()

    for i in range(2):
        now = even if i == 0 else odd
        first = PAIRS - LEAD + 2 * i
        c_copy(first // 2).wait_recv()
        for n in range(2):
            shade_own(first + n, now[1], 2 * n)
        if i == 0:
            layer2(h1b, h2b)
        for n in range(2):
            send_own(first + n)
    for k in range(3):
        hand_on(k)
    put4(xrecv.at[x], merge_z(3))
    wait_for(xrecv.at[pl.ds(0, NX - 1), pl.ds(0, USED)], xr_sem)
    left, right, tleft, tright = ordered([get(xrecv.at[s]) for s in range(NX)])
    color_out[:, :LANES] = left
    color_out[:, LANES:] = right
    light_out[:, :LANES] = tleft
    light_out[:, LANES:] = tright

    wait_for(table_bf.at[pl.ds(0, 384)], ysend_sem)
    wait_for(csend, cs_sem)
    wait_for(zsend.at[:, pl.ds(1, NZ - 1)], zs_sem)
    wait_for(xsend.at[pl.ds(0, NX - 1), pl.ds(0, USED)], xs_sem)


def shards(bricks, pair_index, interp_weight, step_len, sample_count, w_first, w_second, w_out):
    part = functools.partial(pltpu.VMEM, dtype=F32)
    dma = pltpu.SemaphoreType.DMA
    color, light = pl.pallas_call(
        kernel,
        out_shape=(jax.ShapeDtypeStruct((32, RAYS), F32), jax.ShapeDtypeStruct((1, RAYS), F32)),
        in_specs=[pl.BlockSpec(memory_space=pltpu.HBM)] * 8,
        out_specs=[pl.BlockSpec(memory_space=pltpu.VMEM)] * 2,
        scratch_shapes=[
            pltpu.VMEM((512, 512), BF),
            pltpu.SMEM((16, 64), jnp.int32),
            pltpu.VMEM((TILES, 2 * RAYS, LANES), BF),
            pltpu.VMEM((2, TILES * RAYS), F32),
            pltpu.VMEM((1, TILES * RAYS), jnp.int32),
            pltpu.VMEM((64, 256), BF),
            pltpu.VMEM((256, 256), BF),
            pltpu.VMEM((33, 256), BF),
            pltpu.VMEM((256, 256), BF),
            pltpu.VMEM((2, 2 * RAYS, LANES), F32),
            pltpu.VMEM((2, 512, 8, LANES), F32),
        ]
        + [pltpu.VMEM((GROUP * 256, 512), BF)] * 4
        + [part((PAIRS, 2, ROWS, LANES))] * 2
        + [pltpu.VMEM((NX, NZ, 80, LANES), jnp.int16)] * 2
        + [part((NX, ROWS, LANES))] * 2
        + [dma((7,)), dma((CHUNKS,)), dma, dma((6,)), dma, dma((PAIRS // 2,))]
        + [dma, dma((NX,)), dma, dma],
        compiler_params=pltpu.CompilerParams(
            collective_id=0, has_side_effects=True, vmem_limit_bytes=62 * 2**20
        ),
        name="render",
    )(
        bricks,
        jnp.swapaxes(pair_index, 1, 2),
        interp_weight,
        step_len,
        sample_count,
        w_first,
        w_second,
        w_out.T,
    )
    return color, light.reshape(RAYS)


def solution(mesh):
    return jax.shard_map(
        shards,
        mesh=mesh,
        in_specs=(
            P("region", "ray", None),
            P("region", "ray", None),
            P("region", "ray", None, None),
            P("region", None, "ray"),
            P("region", "ray"),
            P(),
            P(),
            P(),
        ),
        out_specs=(P(None, ("ray", "region")), P(("ray", "region"))),
        check_vma=False,
    )
```

time: 45.4 us -> 43.7 us (0.963)
  Pallas kernels: 42 us -> 40.3 us
    pallas_call x1, Pallas kernels: 42 us -> 40.3 us  [shards(): pl.pallas_call(kernel, out_shape=(jax.ShapeDtypeStruct((32, RAYS), F32),...]
where the time goes in v3:
time: 43.7 us; the launch traced here: 43.6 us
  Pallas kernels  40.3 us (92%)
  local copies, waits for them, and re-layouts  2.6 us (6%)
  between operations  0.64 us (1%)
    pallas_call x1, Pallas kernels, shards(): pl.pallas_call(kernel, out_shape=(jax.ShapeDtypeStruct((32, RAYS), F32),...  40.3 us
    unnamed x2, local copies, waits for them, and re-layouts  2.6 us

profile of v3, /device:TPU:1, one launch (start us, length us, event | category | flops | bytes accessed | tf_op | source)
XLA Modules:
  0.0 43.6 jit_solution(16080720200761590251)
XLA Ops:
  0.6 40.3 %render.1 = (f32[32,256]{1,0:T(8,128)}, f32[1,256]{1,0:T(1,128)}) custom-call(bf16[1,128,512]{2,1,0:T(8,128)(2,1)} %bricks.1, s32[1,16,64]{2,1,0:T(8,128)} %bitcast.4, bf16[1,64,512,128]{3,2,1,0:T(8,128)(2,1)} %interp.1, f32[1,2,16384]{2,1,0:T(2,128)} %step_hbm.1, s32[1,16384]{1,0:T(1,128)} %count_hbm.1, bf16[64,256]{1,0:T(8,128)(2,1)} %w1_hbm.1, ...), custom_call_target="tpu_custom_call" | custom-call | tf_op jit(solution)/shard_map/render/pallas_call | solution.py:361
  41.0 1.4 %copy.12 = f32[32,256]{1,0:T(8,128)} copy(f32[32,256]{1,0:T(8,128)} %get-tuple-element.8) | data formatting | bytes 65536
  42.3 1.2 %copy.13 = f32[256]{0:T(256)} copy(f32[256]{0:T(256)} %bitcast.5) | data formatting | bytes 2048

commit v4 on v3

--- a/solution.py
+++ b/solution.py
@@ -22,7 +22,7 @@
 ROWS = 72
 USED = 66
 CHUNKS = 8
-FORWARD = 3
+FORWARD = (2, 3)
 FINE = 2.0**20
 TOP = 32700.0
 
@@ -98,9 +98,6 @@
             ]
         )
     ]
-    for copy in small:
-        copy.start()
-
     def wv_copy(c):
         n = TILES // CHUNKS
         return pltpu.make_async_copy(interp.at[0, pl.ds(c * n, n)], wv.at[pl.ds(c * n, n)], wv_sem.at[c])
@@ -110,32 +107,39 @@
 
     pl.semaphore_wait(barrier, (NY - 1) + 1 + (NZ - 1) + (NX - 1))
 
-    def half_of(owner, h):
-        return table_bf.at[pl.ds(lax.rem(owner + NY, NY) * 128 + h * 64, 64)]
+    def y_rows(owner, first):
+        return table_bf.at[pl.ds(lax.rem(owner + NY, NY) * 128 + first, 32)]
+
+    y_plan = [(y, 0, 1), (y, 64, 3), (y, 32, 1), (y, 96, 3), (y, 64, 1), (y, 0, 3), (y, 96, 1), (y, 32, 3)]
+    y_plan += [(y - 1, 0, 1), (y + 1, 64, 3), (y - 1, 32, 1), (y + 1, 96, 3)]
 
     def y_copy(n):
-        owner, h, to = ((y, 0, 1), (y, 1, 3), (y, 1, 1), (y, 0, 3), (y - 1, 0, 1), (y + 1, 1, 3))[n]
+        owner, first, to = y_plan[n]
         return pltpu.make_async_remote_copy(
-            src_ref=half_of(owner, h) if n >= 4 else bricks.at[0, pl.ds(h * 64, 64)],
-            dst_ref=half_of(owner, h),
+            src_ref=y_rows(owner, first) if n >= 8 else bricks.at[0, pl.ds(first, 32)],
+            dst_ref=y_rows(owner, first),
             send_sem=ysend_sem,
             recv_sem=yrecv_sem.at[n],
             device_id={"ray": lax.rem(y + to, NY)},
             device_id_type=MESH,
         )
 
-    for n in range(4):
+    for n in range(8):
         y_copy(n).start()
+
+    for copy in small:
+        copy.start()
 
     for copy in small:
         copy.wait()
     w2t[...] = w2[...].astype(F32).T.astype(BF)
 
     for c in range(CHUNKS):
-        if c == FORWARD:
+        if c in FORWARD:
             for n in range(2):
+                n += 2 * FORWARD.index(c)
                 y_copy(n).wait_recv()
-                y_copy(4 + n).start()
+                y_copy(8 + n).start()
         wv_copy(c).wait()
 
         @pl.loop(0, TILES // CHUNKS)
@@ -146,18 +150,23 @@
             wv[t, 0:RAYS] = stage[b, pl.ds(0, RAYS, stride=2), :].astype(BF)
             wv[t, RAYS : 2 * RAYS] = stage[b, pl.ds(1, RAYS, stride=2), :].astype(BF)
 
-    for n in range(2, 6):
-        y_copy(n).wait_recv()
-
     half = w1[...]
     none = jnp.zeros_like(half)
     wide = [jnp.concatenate([half, none], 0), jnp.concatenate([none, half], 0)]
-    for v in range(8):
-        cols = (v // 2) * LANES
-        got = jnp.dot(table_bf[:, cols : cols + LANES], wide[v % 2], preferred_element_type=F32)
-        flat = table.reshape(2, 4096, LANES)
-        flat[0, pl.ds(v, 512, stride=8), :] = got[:, :LANES]
-        flat[1, pl.ds(v, 512, stride=8), :] = got[:, LANES:]
+    flat = table.reshape(2, 4096, LANES)
+
+    def fold(owner):
+        first = pl.multiple_of(lax.rem(owner + NY, NY) * 128, 128)
+        for v in range(8):
+            block = table_bf[pl.ds(first, 128), v // 2 * LANES : v // 2 * LANES + LANES]
+            got = jnp.dot(block, wide[v % 2], preferred_element_type=F32)
+            for h in range(2):
+                flat[h, pl.ds(first * 8 + v, 128, stride=8), :] = got[:, h * LANES : (h + 1) * LANES]
+
+    for owner, arrivals in ((y, ()), (y - 1, (4, 6)), (y + 1, (5, 7)), (y + 2, (8, 9, 10, 11))):
+        for n in arrivals:
+            y_copy(n).wait_recv()
+        fold(owner)
 
     def offsets(p):
         j = lax.rem(p, 4)
@@ -380,7 +389,7 @@
         + [part((PAIRS, 2, ROWS, LANES))] * 2
         + [pltpu.VMEM((NX, NZ, 80, LANES), jnp.int16)] * 2
         + [part((NX, ROWS, LANES))] * 2
-        + [dma((7,)), dma((CHUNKS,)), dma, dma((6,)), dma, dma((PAIRS // 2,))]
+        + [dma((7,)), dma((CHUNKS,)), dma, dma((12,)), dma, dma((PAIRS // 2,))]
         + [dma, dma((NX,)), dma, dma],
         compiler_params=pltpu.CompilerParams(
             collective_id=0, has_side_effects=True, vmem_limit_bytes=62 * 2**20

time: 43.7 us -> 43 us (0.984)
  Pallas kernels: 40.3 us -> 39.5 us
    pallas_call x1, Pallas kernels: 40.3 us -> 39.5 us  [shards(): pl.pallas_call(kernel, out_shape=(jax.ShapeDtypeStruct((32, RAYS), F32),...]
where the time goes in v4:
time: 43 us; the launch traced here: 42.8 us
  Pallas kernels  39.5 us (92%)
  local copies, waits for them, and re-layouts  2.6 us (6%)
  between operations  0.64 us (1%)
    pallas_call x1, Pallas kernels, shards(): pl.pallas_call(kernel, out_shape=(jax.ShapeDtypeStruct((32, RAYS), F32),...  39.5 us
    unnamed x2, local copies, waits for them, and re-layouts  2.6 us

profile of v4, /device:TPU:1, one launch (start us, length us, event | category | flops | bytes accessed | tf_op | source)
XLA Modules:
  0.0 42.8 jit_solution(13841667429220957711)
XLA Ops:
  0.6 39.5 %render.1 = (f32[32,256]{1,0:T(8,128)}, f32[1,256]{1,0:T(1,128)}) custom-call(bf16[1,128,512]{2,1,0:T(8,128)(2,1)} %bricks.1, s32[1,16,64]{2,1,0:T(8,128)} %bitcast.4, bf16[1,64,512,128]{3,2,1,0:T(8,128)(2,1)} %interp.1, f32[1,2,16384]{2,1,0:T(2,128)} %step_hbm.1, s32[1,16384]{1,0:T(1,128)} %count_hbm.1, bf16[64,256]{1,0:T(8,128)(2,1)} %w1_hbm.1, ...), custom_call_target="tpu_custom_call" | custom-call | tf_op jit(solution)/shard_map/render/pallas_call | solution.py:370
  40.2 1.4 %copy.12 = f32[32,256]{1,0:T(8,128)} copy(f32[32,256]{1,0:T(8,128)} %get-tuple-element.8) | data formatting | bytes 65536
  41.5 1.2 %copy.13 = f32[256]{0:T(256)} copy(f32[256]{0:T(256)} %bitcast.5) | data formatting | bytes 2048

commit v5 on v4

--- a/solution.py
+++ b/solution.py
@@ -344,10 +344,12 @@
         c_copy(first // 2).wait_recv()
         for n in range(2):
             shade_own(first + n, now[1], 2 * n)
+            if i == 1:
+                send_own(first + n)
         if i == 0:
             layer2(h1b, h2b)
-        for n in range(2):
-            send_own(first + n)
+            for n in range(2):
+                send_own(first + n)
     for k in range(3):
         hand_on(k)
     put4(xrecv.at[x], merge_z(3))

time: 43 us -> 43 us (level)
  no operation moved by 1% of the time
where the time goes in v5:
time: 43 us; the launch traced here: 42.8 us
  Pallas kernels  39.6 us (92%)
  local copies, waits for them, and re-layouts  2.6 us (6%)
  between operations  0.64 us (1%)
    pallas_call x1, Pallas kernels, shards(): pl.pallas_call(kernel, out_shape=(jax.ShapeDtypeStruct((32, RAYS), F32),...  39.6 us
    unnamed x2, local copies, waits for them, and re-layouts  2.6 us

profile of v5, /device:TPU:1, one launch (start us, length us, event | category | flops | bytes accessed | tf_op | source)
XLA Modules:
  0.0 42.8 jit_solution(12185234223860625905)
XLA Ops:
  0.6 39.6 %render.1 = (f32[32,256]{1,0:T(8,128)}, f32[1,256]{1,0:T(1,128)}) custom-call(bf16[1,128,512]{2,1,0:T(8,128)(2,1)} %bricks.1, s32[1,16,64]{2,1,0:T(8,128)} %bitcast.4, bf16[1,64,512,128]{3,2,1,0:T(8,128)(2,1)} %interp.1, f32[1,2,16384]{2,1,0:T(2,128)} %step_hbm.1, s32[1,16384]{1,0:T(1,128)} %count_hbm.1, bf16[64,256]{1,0:T(8,128)(2,1)} %w1_hbm.1, ...), custom_call_target="tpu_custom_call" | custom-call | tf_op jit(solution)/shard_map/render/pallas_call | solution.py:372
  40.2 1.4 %copy.12 = f32[32,256]{1,0:T(8,128)} copy(f32[32,256]{1,0:T(8,128)} %get-tuple-element.8) | data formatting | bytes 65536
  41.6 1.2 %copy.13 = f32[256]{0:T(256)} copy(f32[256]{0:T(256)} %bitcast.5) | data formatting | bytes 2048
